TPU v7x, 512 devices: a whole 4x4x16 slice. The times are simulated.
512 devices in a mesh: tm: 64 (over z, x_hi, core), rows: 8 (over x_lo, y).
Axes of the slice: x: 4 (x_hi: 2, x_lo: 2; x = x_hi * 2 + x_lo), y: 4, z: 16, core: 2. Of those that a mesh axis runs over, the one named last changes fastest.
Arguments:
- right_side: float32 [192, 16384], P('tm'), as said below
- aux_field: float32 [192, 16384], P('tm'), may hold values from -0.3 to 0.3
- hopping: float32 [16384, 16384], P('rows', 'tm'), as said below
Outputs:
- solution: float32 [192, 16384], P('tm')
- residual: float32 [192, 16384], P('tm')
Inputs may be any that keep to these rules, and one draw needn't show every extreme that they name: `right_side`: float entries, no structure promised. `hopping`: dense float entries, no structure promised.
All inputs are finite; a program needn't handle non-finite values.
Results may differ from a plain program's by a relative error of at most 0.00028.
Values sent between devices are 32-bit elements; how exact they have to be, the bound alone decides.
A program may use at most 64 MiB of HBM per device.

v0:
```python
import jax
import jax.numpy as jnp
from jax import lax
from jax.sharding import PartitionSpec as P

ITERS = 2


def from_behind(value, axis, steps):
    count = lax.axis_size(axis)
    pairs = [(source, (source + steps) % count) for source in range(count)]
    return lax.ppermute(value, axis, pairs)


def apply_normal(direction, exp_field, hopping):
    time_index = lax.axis_index("tm")
    last_index = lax.axis_size("tm") - 1
    row_index = lax.axis_index("rows")
    row_width = hopping.shape[0]
    edge_row = from_behind(direction[-1:], "tm", 1)
    edge_row = jnp.where(time_index == 0, -edge_row, edge_row)
    outgoing = jnp.concatenate([edge_row, direction[:-1]], axis=0)
    columns = lax.all_to_all(outgoing, "tm", split_axis=1, concat_axis=0, tiled=True)
    applied = lax.psum_scatter(
        lax.dot_general(
            columns,
            hopping,
            (((1,), (1,)), ((), ())),
            precision=lax.Precision.HIGHEST,
            preferred_element_type=jnp.float32,
        ),
        "tm",
        scatter_dimension=0,
        tiled=True,
    )
    offset = row_index * row_width
    own_block = lax.dynamic_slice_in_dim(direction, offset, row_width, 1)
    scaling = lax.dynamic_slice_in_dim(exp_field, offset, row_width, 1)
    mapped = own_block - scaling * applied
    weighted = scaling * mapped
    head_row = from_behind(weighted[:1], "tm", -1)
    head_row = jnp.where(time_index == last_index, -head_row, head_row)
    weighted = jnp.concatenate([weighted[1:], head_row], axis=0)
    partial_cols = jnp.dot(
        lax.all_gather(weighted, "tm", axis=0, tiled=True),
        hopping,
        precision=lax.Precision.HIGHEST,
        preferred_element_type=jnp.float32,
    )
    summed = lax.psum(partial_cols, "rows")
    returned = lax.all_to_all(summed, "tm", split_axis=0, concat_axis=1, tiled=True)
    full_rows = lax.all_gather(mapped, "rows", axis=1, tiled=True)
    return full_rows - returned


def squares(vector):
    return lax.psum(jnp.sum(vector * vector), "tm")


def per_device(right_side, aux_field, hopping):
    exp_field = jnp.exp(aux_field)
    solution = jnp.zeros_like(right_side)
    residual = right_side
    direction = right_side
    norm_now = squares(residual)
    for iteration in range(ITERS):
        image = apply_normal(direction, exp_field, hopping)
        curvature = lax.psum(jnp.sum(direction * image), "tm")
        step_size = norm_now / curvature
        solution = solution + step_size * direction
        residual = residual - step_size * image
        norm_next = squares(residual)
        direction = residual + norm_next / norm_now * direction
        norm_now = norm_next
    return (solution, residual)


def solution(mesh):
    in_specs = (P("tm", None), P("tm", None), P("rows", "tm"))
    out_specs = (P("tm", None), P("tm", None))
    return jax.shard_map(
        per_device, mesh=mesh, in_specs=in_specs, out_specs=out_specs, check_vma=False
    )
```

profile of v0, /device:TPU:1, one launch (start us, length us, event | category | flops | bytes accessed | tf_op | source)
XLA Modules:
  0.0 2131.4 jit_solution(13308072043139808538)
XLA Ops:
  8.4 6.0 collective-permute-start
  18.1 40.8 %all_to_all.76 = f32[3,64,256]{2,0,1:T(4,128)S(1)} all-to-all(f32[3,64,256]{2,0,1:T(4,128)S(1)} %bitcast.24), channel_id=1, replica_groups=mesh['tm'=64,'rows'=8] {'tm'}, dimensions={1} | all-to-all | bytes 393216 | tf_op jit(solution)/shard_map/all_to_all | solution.py:23
  59.0 3.5 fusion.6
  64.5 519.3 %all-reduce.12.cloned.1.call-done = f32[192,2048]{1,0:T(8,128)} async-done(((f32[192,2048]{1,0:T(8,128)}), f32[192,2048]{1,0:T(8,128)}) %all-reduce.12.cloned.1.call-update) | async-done | bytes 1572880
  587.3 3.9 collective-permute-done.1
  591.9 144.4 %all-gather.5.cloned.1.call-done = f32[64,3,2048]{2,1,0:T(4,128)} async-done(((f32[1,3,2048]{2,1,0:T(4,128)}), f32[64,3,2048]{2,1,0:T(4,128)}) %all-gather.5.cloned.1.call-update) | async-done | bytes 1572880 | tf_op jit(solution)/shard_map/all_gather | solution.py:45
  736.4 3.7 reshape.17
  740.1 2.9 fusion.7
  743.9 78.5 %all-reduce.8.cloned.1.call-done = f32[64,3,256]{2,1,0:T(4,128)} async-done(((f32[64,3,256]{2,1,0:T(4,128)}), f32[64,3,256]{2,1,0:T(4,128)}) %all-reduce.8.cloned.1.call-update) | async-done | bytes 196624 | tf_op jit(solution)/shard_map/psum | solution.py:50
  822.4 20.5 all-to-all-start.1
  842.9 23.9 %all_gather.12 = f32[3,16384]{1,0:T(4,128)S(1)} all-gather(f32[3,2048]{1,0:T(4,128)S(1)} %get-tuple-element.12), channel_id=1, replica_groups=mesh['tm'=64,'rows'=8] {'rows'}, dimensions={1}, use_global_device_ids=true | all-gather | bytes 221184 | tf_op jit(solution)/shard_map/all_gather | solution.py:52
  867.6 134.1 %all-reduce.2 = (f32[]{:T(128)}, f32[]{:T(128)}) all-reduce(f32[]{:T(128)} %get-tuple-element.3, f32[]{:T(128)} %get-tuple-element.2), channel_id=1, replica_groups=mesh['tm'=64,'rows'=8] {'tm'}, use_global_device_ids=true, to_apply=%region_1.0 | all-reduce | flops 2 | bytes 16 | tf_op jit(solution)/shard_map/psum | solution.py:57
  1003.7 129.5 %psum.45 = f32[]{:T(128)} all-reduce(f32[]{:T(128)} %multiply_reduce_fusion.1), channel_id=1, replica_groups=mesh['tm'=64,'rows'=8] {'tm'}, use_global_device_ids=true, to_apply=%region_7.8 | all-reduce | flops 1 | bytes 8 | tf_op jit(solution)/shard_map/psum | solution.py:57
  1138.2 42.1 %all_to_all.77 = f32[3,64,256]{2,0,1:T(4,128)S(1)} all-to-all(f32[3,64,256]{2,0,1:T(4,128)S(1)} %bitcast.25), channel_id=1, replica_groups=mesh['tm'=64,'rows'=8] {'tm'}, dimensions={1} | all-to-all | bytes 393216 | tf_op jit(solution)/shard_map/all_to_all | solution.py:23
  1180.4 3.5 fusion.8
  1184.0 518.9 %all-reduce.14.cloned.1.call-done = f32[192,2048]{1,0:T(8,128)} async-done(((f32[192,2048]{1,0:T(8,128)}), f32[192,2048]{1,0:T(8,128)}) %all-reduce.14.cloned.1.call-update) | async-done | bytes 1572880
  1706.5 3.9 collective-permute-done.3
  1711.3 144.3 %all-gather.7.cloned.1.call-done = f32[64,3,2048]{2,1,0:T(4,128)} async-done(((f32[1,3,2048]{2,1,0:T(4,128)}), f32[64,3,2048]{2,1,0:T(4,128)}) %all-gather.7.cloned.1.call-update) | async-done | bytes 1572880 | tf_op jit(solution)/shard_map/all_gather | solution.py:45
  1855.5 3.7 reshape.19
  1859.3 2.9 fusion.9
  1863.0 78.5 %all-reduce.10.cloned.1.call-done = f32[64,3,256]{2,1,0:T(4,128)} async-done(((f32[64,3,256]{2,1,0:T(4,128)}), f32[64,3,256]{2,1,0:T(4,128)}) %all-reduce.10.cloned.1.call-update) | async-done | bytes 196624 | tf_op jit(solution)/shard_map/psum | solution.py:50
  1941.5 20.5 all-to-all-start.3
  1962.0 23.9 %all_gather.14 = f32[3,16384]{1,0:T(4,128)S(1)} all-gather(f32[3,2048]{1,0:T(4,128)S(1)} %get-tuple-element.9), channel_id=1, replica_groups=mesh['tm'=64,'rows'=8] {'rows'}, dimensions={1}, use_global_device_ids=true | all-gather | bytes 221184 | tf_op jit(solution)/shard_map/all_gather | solution.py:52
  1987.3 134.1 %psum.47 = f32[]{:T(128)} all-reduce(f32[]{:T(128)} %get-tuple-element.6), channel_id=1, replica_groups=mesh['tm'=64,'rows'=8] {'tm'}, use_global_device_ids=true, to_apply=%region_11.12 | all-reduce | flops 1 | bytes 8 | tf_op jit(solution)/shard_map/psum | solution.py:68
  (51 shorter events, 25.2 us)
Async XLA Ops:
  7.2 51.8 %copy-start = (f32[2048,256]{1,0:T(8,128)S(1)}, f32[2048,256]{1,0:T(8,128)}, u32[]{:S(2)}) copy-start(f32[2048,256]{1,0:T(8,128)} %param.5) | copy-start | bytes 6291460
  7.2 576.6 %all-reduce.12.cloned.1.call-start = ((), (), s32[]{:S(2)}) async-start(), calls=%async_computation.8 | async-start | bytes 3145728
  8.4 9.5 collective-permute-start
  62.5 521.3 %copy-start.1 = (f32[3,16384]{1,0:T(4,128)S(1)}, f32[3,16384]{1,0:T(4,128)}, u32[]{:S(2)}) copy-start(f32[3,16384]{1,0:T(4,128)} %param.3) | copy-start | bytes 589828
  62.5 673.9 %all-gather.5.cloned.1.call-start = ((), (), s32[]{:S(2)}) async-start(), calls=%async_computation.6 | async-start | bytes 2129920 | tf_op jit(solution)/shard_map/all_gather | solution.py:45
  584.7 6.5 collective-permute-start.1
  591.9 230.5 %all-reduce.8.cloned.1.call-start = ((), (), s32[]{:S(2)}) async-start(), calls=%async_computation.4 | async-start | bytes 524288 | tf_op jit(solution)/shard_map/psum | solution.py:50
  822.4 44.5 %all-to-all-start.1 = ((f32[64,3,256]{2,1,0:T(4,128)}), f32[64,3,256]{2,1,0:T(4,128)S(1)}, u32[]{:S(2)}, u32[]{:S(2)}) async-start(f32[64,3,256]{2,1,0:T(4,128)} %all-reduce.8.cloned.1.call-done), calls=%async_computation.1 | async-start | bytes 524288 | tf_op jit(solution)/shard_map/all_to_all | solution.py:51
  842.8 860.1 %all-reduce.14.cloned.1.call-start = ((), (), s32[]{:S(2)}) async-start(), calls=%async_computation.9 | async-start | bytes 3145728
  1134.7 3.3 collective-permute-start.2
  1183.9 671.6 %all-gather.7.cloned.1.call-start = ((), (), s32[]{:S(2)}) async-start(), calls=%async_computation.7 | async-start | bytes 2129920 | tf_op jit(solution)/shard_map/all_gather | solution.py:45
  1703.9 6.5 collective-permute-start.3
  1711.0 230.5 %all-reduce.10.cloned.1.call-start = ((), (), s32[]{:S(2)}) async-start(), calls=%async_computation.5 | async-start | bytes 524288 | tf_op jit(solution)/shard_map/psum | solution.py:50
  1941.5 44.4 %all-to-all-start.3 = ((f32[64,3,256]{2,1,0:T(4,128)}), f32[64,3,256]{2,1,0:T(4,128)S(1)}, u32[]{:S(2)}, u32[]{:S(2)}) async-start(f32[64,3,256]{2,1,0:T(4,128)} %all-reduce.10.cloned.1.call-done), calls=%async_computation.3 | async-start | bytes 524288 | tf_op jit(solution)/shard_map/all_to_all | solution.py:51
Sparse Core Ops, SparseCore 0:
  62.6 521.1 all-reduce.11
  592.0 144.3 all-gather.4
  744.0 78.3 all-reduce.7
  1184.0 518.8 all-reduce.13
  1711.1 144.3 all-gather.6
  1863.1 78.3 all-reduce.9
where the time goes:
time: 2130 us
  waiting for transfers between devices  1500 us (70%)
  blocking collectives  528 us (25%)
  starting transfers between devices  54.5 us (3%)
    unnamed x8, waiting for transfers between devices  1040 us
    all_gather x2, waiting for transfers between devices, apply_normal(): lax.all_gather(weighted, 'tm', axis=0, tiled=True)  289 us
    psum x2, blocking collectives, squares(): return lax.psum(jnp.sum(vector * vector), 'tm')  264 us
    psum x2, waiting for transfers between devices, apply_normal(): summed = lax.psum(partial_cols, 'rows')  157 us
    psum x1, blocking collectives, per_device(): curvature = lax.psum(jnp.sum(direction * image), 'tm')  134 us
    all_to_all x2, blocking collectives, apply_normal(): lax.all_to_all(outgoing, 'tm', split_axis=1, concat_axis=0, tiled=True)  82.9 us
    all_gather x2, blocking collectives, apply_normal(): full_rows = lax.all_gather(mapped, 'rows', axis=1, tiled=True)  47.9 us
  transfers between devices with their start and end apart: 12, of which 10 were waited for; matrix products, arithmetic and copies ran while one was open for 0% of the time, Pallas kernels for 0%

commit v1 on v0

v1 whole, which is shorter than its diff:
```python
import functools

import jax
import jax.numpy as jnp
from jax import lax
from jax.experimental import pallas as pl
from jax.experimental.pallas import tpu as pltpu
from jax.sharding import PartitionSpec as P

SR = 8
F32 = jnp.float32
BF16 = jnp.bfloat16


def split(value):
    high = value.astype(BF16)
    return high, (value - high.astype(F32)).astype(BF16)


def product(a_high, a_low, b_high, b_low):
    dot = functools.partial(jnp.dot, preferred_element_type=F32)
    return dot(a_high, b_high) + (dot(a_low, b_high) + dot(a_high, b_low))


def fold(value, width):
    squared = value * value
    rows = squared.shape[0]
    tile = squared.reshape(rows // SR, SR, squared.shape[1]).sum(axis=0)
    out = tile[:, :width]
    for start in range(width, squared.shape[1], width):
        out = out + tile[:, start : start + width]
    return out


def total(tile):
    return jnp.sum(jnp.sum(tile, axis=0, keepdims=True), axis=1, keepdims=True)


def arrived(ref, sem):
    pltpu.make_async_copy(ref, ref, sem).wait()


def kernel(
    tm, rows, b_ref, aux_ref, h_ref, x_out, r_out,
    hf_hi, hf_lo, hb_hi, hb_lo,
    b_in, aux_in, b_piece, r_piece, e_send, einv_send, e_mid, e_diag,
    v_full, v_hi, v_lo, v_fold, part, sib_in, right_in, left_in, x_buf, x_in,
    q_mid, gath, acc, c_acc, rs_send, rs_in, out_send, out_mid,
    b_sem, aux_sem, ag_sem, emid_sem, ediag_sem,
    fsib_sem, fr_sem, fl_sem, fx_sem, br_sem, bl_sem, bsib_sem, rs_sem,
    tr_sem, fin_sem, init_send, ag_send, emid_send, ediag_send,
    fsib_send, fr_send, fl_send, fx_send, br_send, bl_send, bsib_send, rs_send_sem,
    tr_send, fin_send, loc_sem,
):
    m = lax.axis_index("tm")
    r = lax.axis_index("rows")
    z = m // 4
    core = m % 2
    other = 1 - core
    nz = tm // 4
    nr, nl = nz // 2, nz // 2 - 1
    g = tm // rows
    steps = b_ref.shape[0]
    t_all = steps * tm
    tg, ht = t_all // rows, t_all // 2
    cw = h_ref.shape[1]
    rw = h_ref.shape[0]
    w = rw // nz
    zper = cw // w
    half_rows = rows // 2
    is_diag = r == m // g

    sibling = (m + 1 - 2 * core, r)
    x_other = (m + 2 - 4 * ((m // 2) % 2), r)
    right = (lax.rem(m + 4, tm), r)
    left = (lax.rem(m + tm - 4, tm), r)

    def send(src, dst, ssem, rsem, device):
        pltpu.make_async_remote_copy(
            src_ref=src, dst_ref=dst, send_sem=ssem, recv_sem=rsem,
            device_id=device, device_id_type=pl.DeviceIdType.MESH,
        ).start()

    nxt = lax.rem(r + 1, rows)
    mine = lax.rem(m, g)
    for k in range(g):
        target = (nxt * g + k, m // g)
        cols = pl.ds(pl.multiple_of((nxt * g + k) * cw, cw), cw)
        send(b_ref.at[:, cols], b_in.at[mine], init_send.at[0, k], b_sem.at[mine], target)
    for k in range(g):
        target = (nxt * g + k, m // g)
        cols = pl.ds(pl.multiple_of((nxt * g + k) * cw, cw), cw)
        send(aux_ref.at[:, cols], aux_in.at[mine], init_send.at[1, k], aux_sem.at[mine], target)

    def prepare(chunk, carry):
        block = h_ref[pl.ds(pl.multiple_of(chunk * w, w), w), :]
        high, low = split(block)
        hb_hi[chunk] = high
        hb_lo[chunk] = low
        high, low = split(block.T)
        hf_hi[chunk] = high
        hf_lo[chunk] = low
        return carry

    lax.fori_loop(0, nz, prepare, 0)

    def spread(source, it):
        for d in range(1, rows):
            send(source, v_full.at[it, r], ag_send.at[it], ag_sem.at[it], (m, lax.rem(r + d, rows)))

    for i in range(g):
        arrived(b_in.at[i], b_sem.at[i])
        b_piece[steps * i : steps * (i + 1), :] = b_in[i]
    spread(b_piece, 0)
    v_full[0, r] = b_piece[...]

    for i in range(g):
        arrived(aux_in.at[i], aux_sem.at[i])
        value = aux_in[i]
        einv_send[steps * i : steps * (i + 1), :] = jnp.exp(-value)
        grown = jnp.exp(value)
        for h in range(zper):
            e_send[h, steps * i : steps * (i + 1), :] = grown[:, h * w : (h + 1) * w]

    for h in range(zper):
        for xh in range(2):
            to_m = (zper * mine + h) * 4 + xh * 2 + r // half_rows
            to_r = m // g
            same = jnp.logical_and(to_m == m, to_r == r)
            sem = emid_sem.at[lax.rem(r, half_rows)]

            @pl.when(same)
            def _():
                pltpu.make_async_copy(e_send.at[h], e_mid.at[lax.rem(r, half_rows)], sem).start()

            @pl.when(jnp.logical_not(same))
            def _():
                send(e_send.at[h], e_mid.at[lax.rem(r, half_rows)], emid_send.at[h, xh], sem, (to_m, to_r))

    @pl.when(is_diag)
    def _():
        e_diag[r] = einv_send[...]

    @pl.when(jnp.logical_not(is_diag))
    def _():
        send(einv_send, e_diag.at[r], ediag_send.at[0], ediag_sem.at[0], (m, m // g))

    row_id = lax.broadcasted_iota(jnp.int32, (t_all, 1), 0)

    def forward(it):
        v = v_full[it].reshape(t_all, cw)
        shifted = pltpu.roll(v, 1, 0)
        shifted = jnp.where(row_id == 0, -shifted, shifted)
        high, low = split(shifted)
        v_hi[...] = high
        v_lo[...] = low
        squares = fold(v, w)

        @pl.when(is_diag)
        def _():
            if it == 0:
                arrived(e_diag.at[pl.ds(0, rows - 1)], ediag_sem.at[0])
            inverse = e_diag[...].reshape(t_all, cw) * v
            for h in range(zper):
                v_fold[h] = inverse[:, h * w : (h + 1) * w]

        def compute(k):
            chunk = lax.rem(z + k, nz)
            value = product(v_hi[...], v_lo[...], hf_hi[chunk], hf_lo[chunk])
            part[it, k, 0, :ht, :] = value[:ht]
            part[it, k, 1, :ht, :] = value[ht:]
            part[it, k, 0, ht:, :] = squares
            part[it, k, 1, ht:, :] = squares

            @pl.when(jnp.logical_and(is_diag, chunk // zper == mine))
            def _():
                own = v_fold[lax.rem(chunk, zper)]
                part[it, k, 0, :ht, :] -= own[:ht]
                part[it, k, 1, :ht, :] -= own[ht:]

            send(part.at[it, k, other], sib_in.at[it, k], fsib_send.at[it], fsib_sem.at[it, k], sibling)

        compute(nr)
        compute(nr + 1)

        def step(s, carry):
            @pl.when(s < nr)
            def _():
                compute(nr - s)
                compute(lax.rem(nr + 1 + s, nz))

            k = nr + 1 - s
            arrived(sib_in.at[it, k], fsib_sem.at[it, k])
            part[it, k, core] += sib_in[it, k]

            @pl.when(s > 1)
            def _():
                arrived(right_in.at[it, s - 2], fr_sem.at[it, s - 2])
                part[it, k, core] += right_in[it, s - 2]

            send(part.at[it, k, core], right_in.at[it, s - 1], fr_send.at[it], fr_sem.at[it, s - 1], right)

            @pl.when(s <= nl)
            def _():
                k = nr + s
                arrived(sib_in.at[it, k], fsib_sem.at[it, k])
                part[it, k, core] += sib_in[it, k]

                @pl.when(s > 1)
                def _():
                    arrived(left_in.at[it, s - 2], fl_sem.at[it, s - 2])
                    part[it, k, core] += left_in[it, s - 2]

                send(part.at[it, k, core], left_in.at[it, s - 1], fl_send.at[it], fl_sem.at[it, s - 1], left)

            return carry

        lax.fori_loop(1, nr + 1, step, 0)
        arrived(sib_in.at[it, 0], fsib_sem.at[it, 0])
        arrived(left_in.at[it, nl - 1], fl_sem.at[it, nl - 1])
        arrived(right_in.at[it, nr - 1], fr_sem.at[it, nr - 1])
        own = part[it, 0, core] + sib_in[it, 0] + (left_in[it, nl - 1] + right_in[it, nr - 1])
        x_buf[it] = own
        send(x_buf.at[it], x_in.at[it], fx_send.at[it], fx_sem.at[it], x_other)
        arrived(x_in.at[it], fx_sem.at[it])
        summed = own + x_in[it]
        return summed[:ht], total(summed[ht:])

    def backward(it, q, e):
        gath[it, 0, core, :ht, :] = e * q
        gath[it, 0, core, ht:, :] = fold(q, w)

        def to_sibling(k):
            send(gath.at[it, k, core], gath.at[it, k, core], bsib_send.at[it], bsib_sem.at[it, k], sibling)

        def to_right(k, s):
            send(gath.at[it, k, core], gath.at[it, lax.rem(k + nz - 1, nz), core],
                 br_send.at[it], br_sem.at[it, s], right)

        def to_left(k, s):
            send(gath.at[it, k, core], gath.at[it, k + 1, core], bl_send.at[it], bl_sem.at[it, s], left)

        to_right(0, 0)
        to_left(0, 0)
        to_sibling(0)
        acc[...] = jnp.zeros_like(acc)
        c_acc[...] = jnp.zeros_like(c_acc)

        def use(k):
            arrived(gath.at[it, k, other], bsib_sem.at[it, k])
            block = jnp.concatenate([gath[it, k, 0, :ht, :], gath[it, k, 1, :ht, :]], axis=0)
            high, low = split(block)
            chunk = lax.rem(z + k, nz)
            acc[...] += product(high, low, hb_hi[chunk], hb_lo[chunk])
            c_acc[...] += gath[it, k, 0, ht:, :] + gath[it, k, 1, ht:, :]

        def step(s, carry):
            k = nz - s
            arrived(gath.at[it, k, core], br_sem.at[it, s - 1])

            @pl.when(s < nr)
            def _():
                to_right(k, s)

            to_sibling(k)

            @pl.when(s <= nl)
            def _():
                arrived(gath.at[it, s, core], bl_sem.at[it, s - 1])

                @pl.when(s < nl)
                def _():
                    to_left(s, s)

                to_sibling(s)

            use(lax.rem(nz - s + 1, nz))

            @pl.when(s > 1)
            def _():
                use(s - 1)

            return carry

        lax.fori_loop(1, nr + 1, step, 0)
        use(nz // 2)

        returned = pltpu.roll(acc[...], t_all - 1, 0)
        acc[...] = jnp.where(row_id == t_all - 1, returned, -returned)

        @pl.when(is_diag)
        def _():
            for h in range(zper):
                k = lax.rem(zper * mine + h + nz - z, nz)
                block = jnp.concatenate([gath[it, k, 0, :ht, :], gath[it, k, 1, :ht, :]], axis=0)
                inverse = e_diag[:, :, h * w : (h + 1) * w].reshape(t_all, w)
                acc[:, h * w : (h + 1) * w] += inverse * block

        for k in range(rows):
            for h in range(zper):
                rs_send[it, k, h * tg : (h + 1) * tg, :] = acc[k * tg : (k + 1) * tg, h * w : (h + 1) * w]
            rs_send[it, k, zper * tg :, :] = c_acc[...]
        for d in range(1, rows):
            to = lax.rem(r + d, rows)
            send(rs_send.at[it, to], rs_in.at[it, r], rs_send_sem.at[it], rs_sem.at[it], (m, to))
        rs_in[it, r] = rs_send[it, r]
        arrived(rs_send.at[it, pl.ds(0, rows - 1)], rs_sem.at[it])
        summed = rs_in[it, 0]
        for k in range(1, rows):
            summed = summed + rs_in[it, k]
        image = jnp.concatenate([summed[h * tg : (h + 1) * tg] for h in range(zper)], axis=1)
        return image, total(summed[zper * tg :])

    arrived(v_full.at[0, pl.ds(0, rows - 1)], ag_sem.at[0])
    summed, norm_0 = forward(0)
    for i in range(half_rows):
        arrived(e_mid.at[i], emid_sem.at[i])
    e = e_mid[...].reshape(ht, w)
    q = -(e * summed)
    q_mid[...] = q
    image, curvature = backward(0, q, e)
    step_0 = norm_0 / curvature
    residual = b_piece[...] - step_0 * image
    r_piece[...] = residual
    spread(r_piece, 1)
    v_full[1, r] = residual
    arrived(v_full.at[1, pl.ds(0, rows - 1)], ag_sem.at[1])

    summed, norm_1 = forward(1)
    beta = norm_1 / norm_0
    e = e_mid[...].reshape(ht, w)
    q = beta * q_mid[...] - e * summed
    image, curvature = backward(1, q, e)
    step_1 = norm_1 / curvature
    b = b_piece[...]
    residual = r_piece[...]
    answer = step_0 * b + step_1 * (residual + beta * b)
    residual = residual - step_1 * image

    for i in range(g):
        out_send[i, 0] = answer[steps * i : steps * (i + 1)]
        out_send[i, 1] = residual[steps * i : steps * (i + 1)]
    to_row = lax.rem(m // g + rows - 1, rows)
    for i in range(g):
        send(out_send.at[i], out_mid.at[mine], tr_send.at[i], tr_sem.at[mine], (g * r + i, to_row))
    for k in range(g):
        arrived(out_mid.at[k], tr_sem.at[k])
    here = pl.multiple_of(nxt * rw, rw)
    for k in range(g):
        x_out[:, pl.ds(here + k * cw, cw)] = out_mid[k, 0]
        r_out[:, pl.ds(here + k * cw, cw)] = out_mid[k, 1]
    block = pl.ds(here, rw)
    for d in range(1, rows):
        to = (m, lax.rem(r + d, rows))
        send(x_out.at[:, block], x_out.at[:, block], fin_send.at[0, d - 1], fin_sem.at[0, d - 1], to)
        send(r_out.at[:, block], r_out.at[:, block], fin_send.at[1, d - 1], fin_sem.at[1, d - 1], to)
    for d in range(1, rows):
        source = lax.rem(r + rows - d, rows)
        there = pl.ds(pl.multiple_of(lax.rem(source + 1, rows) * rw, rw), rw)
        arrived(x_out.at[:, there], fin_sem.at[0, d - 1])
        arrived(r_out.at[:, there], fin_sem.at[1, d - 1])

    for d in range(1, rows):
        arrived(x_out.at[:, block], fin_send.at[0, d - 1])
        arrived(r_out.at[:, block], fin_send.at[1, d - 1])
    for i in range(g):
        arrived(out_send.at[i], tr_send.at[i])
        arrived(b_in.at[i], init_send.at[0, i])
        arrived(aux_in.at[i], init_send.at[1, i])
    for h in range(zper):
        for xh in range(2):
            to_m = (zper * mine + h) * 4 + xh * 2 + r // half_rows
            same = jnp.logical_and(to_m == m, m // g == r)

            @pl.when(jnp.logical_not(same))
            def _():
                arrived(e_send.at[h], emid_send.at[h, xh])

    @pl.when(jnp.logical_not(is_diag))
    def _():
        arrived(einv_send, ediag_send.at[0])

    for it in range(2):
        arrived(v_full.at[it, pl.ds(0, rows - 1)], ag_send.at[it])
        arrived(sib_in.at[it], fsib_send.at[it])
        arrived(right_in.at[it], fr_send.at[it])
        arrived(left_in.at[it], fl_send.at[it])
        arrived(x_in.at[it], fx_send.at[it])
        arrived(right_in.at[it], br_send.at[it])
        arrived(left_in.at[it], bl_send.at[it])
        arrived(sib_in.at[it], bsib_send.at[it])
        arrived(rs_send.at[it, pl.ds(0, rows - 1)], rs_send_sem.at[it])


def per_device(tm, rows, right_side, aux_field, hopping):
    steps = right_side.shape[0]
    t_all = steps * tm
    tg, ht = t_all // rows, t_all // 2
    rw, cw = hopping.shape
    nz = tm // 4
    nr, nl = nz // 2, nz // 2 - 1
    g = tm // rows
    w = rw // nz
    zper = cw // w
    vm = pltpu.VMEM
    dma = pltpu.SemaphoreType.DMA
    scratch = [
        vm((nz, cw, w), BF16), vm((nz, cw, w), BF16), vm((nz, w, cw), BF16), vm((nz, w, cw), BF16),
        vm((g, steps, cw), F32), vm((g, steps, cw), F32), vm((tg, cw), F32), vm((tg, cw), F32),
        vm((zper, tg, w), F32), vm((tg, cw), F32), vm((rows // 2, tg, w), F32), vm((rows, tg, cw), F32),
        vm((2, rows, tg, cw), F32), vm((t_all, cw), BF16), vm((t_all, cw), BF16), vm((zper, t_all, w), F32),
        vm((2, nz, 2, ht + SR, w), F32), vm((2, nz, ht + SR, w), F32),
        vm((2, nr, ht + SR, w), F32), vm((2, nl, ht + SR, w), F32),
        vm((2, ht + SR, w), F32), vm((2, ht + SR, w), F32),
        vm((ht, w), F32), vm((2, nz, 2, ht + SR, w), F32), vm((t_all, cw), F32), vm((SR, w), F32),
        vm((2, rows, zper * tg + SR, w), F32), vm((2, rows, zper * tg + SR, w), F32),
        vm((g, 2, steps, cw), F32), vm((g, 2, steps, cw), F32),
        dma((g,)), dma((g,)), dma((2,)), dma((rows // 2,)), dma((1,)),
        dma((2, nz)), dma((2, nr)), dma((2, nl)), dma((2,)),
        dma((2, nr)), dma((2, nl)), dma((2, nz)), dma((2,)),
        dma((g,)), dma((2, rows)), dma((2, g)), dma((2,)), dma((zper, 2)), dma((1,)),
        dma((2,)), dma((2,)), dma((2,)), dma((2,)), dma((2,)), dma((2,)), dma((2,)), dma((2,)),
        dma((g,)), dma((2, rows)), dma((1,)),
    ]
    out = jax.ShapeDtypeStruct(right_side.shape, F32)
    in_vmem = pl.BlockSpec(memory_space=pltpu.VMEM)
    return pl.pallas_call(
        functools.partial(kernel, tm, rows),
        out_shape=(out, out),
        in_specs=[in_vmem] * 3,
        out_specs=(in_vmem, in_vmem),
        scratch_shapes=scratch,
        compiler_params=pltpu.CompilerParams(has_side_effects=True, vmem_limit_bytes=48 * 1024 * 1024),
        cost_estimate=pl.CostEstimate(
            flops=24 * t_all * rw * cw, bytes_accessed=4 * rw * cw, transcendentals=2 * tg * cw
        ),
    )(right_side, aux_field, hopping)


def solution(mesh):
    in_specs = (P("tm", None), P("tm", None), P("rows", "tm"))
    out_specs = (P("tm", None), P("tm", None))
    call = functools.partial(per_device, mesh.shape["tm"], mesh.shape["rows"])
    return jax.shard_map(call, mesh=mesh, in_specs=in_specs, out_specs=out_specs, check_vma=False)
```

time: 2130 us -> 212 us (0.10)
  waiting for transfers between devices: 1500 us -> 0 us
  blocking collectives: 528 us -> 0 us
  Pallas kernels: 0 us -> 205 us
  starting transfers between devices: 54.5 us -> 0 us
    unnamed x8 -> x0, waiting for transfers between devices: 1040 us -> none
    psum x3 -> x0, blocking collectives: 398 us -> none  [the longest x2 264 us: squares(): return lax.psum(jnp.sum(vector * vector), 'tm')]
    all_gather x2 -> x0, waiting for transfers between devices: 289 us -> none  [apply_normal(): lax.all_gather(weighted, 'tm', axis=0, tiled=True)]
    pallas_call x0 -> x1, Pallas kernels: none -> 205 us  [per_device(): pl.pallas_call(functools.partial(kernel, tm, rows), out_shape=(out, out),...]
    psum x2 -> x0, waiting for transfers between devices: 157 us -> none  [apply_normal(): summed = lax.psum(partial_cols, 'rows')]
    all_to_all x2 -> x0, blocking collectives: 82.9 us -> none  [apply_normal(): lax.all_to_all(outgoing, 'tm', split_axis=1, concat_axis=0, tiled=True)]
    all_gather x2 -> x0, blocking collectives: 47.9 us -> none  [apply_normal(): full_rows = lax.all_gather(mapped, 'rows', axis=1, tiled=True)]
    all_to_all x2 -> x0, starting transfers between devices: 40.9 us -> none  [apply_normal(): lax.all_to_all(summed, 'tm', split_axis=0, concat_axis=1, tiled=True)]
  transfers between devices with their start and end apart: 12 -> 0, of which waited for: 10 -> 0; matrix products, arithmetic and copies ran while one was open for 0% -> 0% of each run, Pallas kernels for 0% -> 0%
where the time goes in v1:
time: 212 us; the launch traced here: 211 us
  Pallas kernels  205 us (97%)
  local copies, waits for them, and re-layouts  4.89 us (2%)
    pallas_call x1, Pallas kernels, per_device(): pl.pallas_call(functools.partial(kernel, tm, rows), out_shape=(out, out),...  205 us
    unnamed x8, local copies, waits for them, and re-layouts  4.89 us

profile of v1, /device:TPU:1, one launch (start us, length us, event | category | flops | bytes accessed | tf_op | source)
XLA Modules:
  0.0 210.9 jit_solution(6295542613312740981)
XLA Ops:
  0.6 0.0 copy-start
  0.6 1.6 copy-done
  2.2 0.0 copy-start.1
  2.2 0.9 copy-done.1
  3.2 0.0 copy-start.2
  3.2 0.9 copy-done.2
  4.1 205.3 %shard_map.50 = (f32[3,16384]{1,0:T(4,128)S(1)}, f32[3,16384]{1,0:T(4,128)S(1)}) custom-call(f32[3,16384]{1,0:T(4,128)S(1)} %copy-done.1, f32[3,16384]{1,0:T(4,128)S(1)} %copy-done.2, f32[2048,256]{1,0:T(8,128)S(1)} %copy-done), custom_call_target="tpu_custom_call" | custom-call | flops 2415919104 | bytes 2097152 | tf_op jit(solution)/shard_map/pallas_call | solution.py:427
  209.5 0.7 copy.7
  210.2 0.7 copy.8
Async XLA Ops:
  0.6 1.6 copy-start
  2.2 0.9 copy-start.1
  3.2 0.9 copy-start.2
